TPU v7x, 512 devices: a whole 4x8x8 slice. The times are simulated.
512 devices in a mesh: row: 8 (over y), col: 16 (over x_lo, z), layer: 4 (over x_hi, core).
Axes of the slice: x: 4 (x_hi: 2, x_lo: 2; x = x_hi * 2 + x_lo), y: 8, z: 8, core: 2. Of those that a mesh axis runs over, the one named last changes fastest.
Arguments:
- integrals: bfloat16 [64, 1024, 3072], P('layer', 'col', 'row'), may hold values from -0.0234375 to 0.0234375
- amplitudes: bfloat16 [64, 1024, 2048], P('layer', 'row', 'col'), may hold values from -6 to 6
- coulomb: bfloat16 [3072, 2048], P(('row', 'layer'), 'col'), may hold values from -6 to 6
- row_gap: float32 [3072], P(('row', 'layer')), may hold values from 0.5 to 4
- col_gap: float32 [2048], P('col'), may hold values from 0.5 to 4
Outputs:
- residual: float32 [3072, 2048], P(('row', 'layer'), 'col')
All inputs are finite; a program needn't handle non-finite values.
Results may differ from a plain program's by a relative error of at most 0.0003.
Values may be sent and summed in bfloat16 or wider, within the bound.
No kernel may reach another device: no remote copies, remote signals or barrier semaphores. Data moves between devices by JAX's collectives and lax.ppermute only.
A program may use at most 64 MiB of HBM per device.

v0:
```python
import jax
import jax.numpy as jnp
from jax import lax
from jax.sharding import PartitionSpec as P


def local(integrals, amplitudes, coulomb, row_gap, col_gap):
    contract = (((0, 1), (0, 1)), ((), ()))
    gathered = lax.all_gather(amplitudes, "row", axis=1, tiled=True)
    partial_sum = lax.dot_general(
        lax.all_gather(integrals, "col", axis=1, tiled=True),
        gathered,
        contract,
        preferred_element_type=jnp.float32,
    )
    share_rows = coulomb.shape[0]
    summed_all = lax.psum(partial_sum, "layer")
    own_rows = lax.dynamic_slice_in_dim(
        summed_all, lax.axis_index("layer") * share_rows, share_rows, 0
    )
    gap_sum = row_gap[:, None] + col_gap[None, :]
    return (coulomb.astype(jnp.float32) + own_rows) / gap_sum


def solution(mesh):
    placed = (
        P("layer", "col", "row"),
        P("layer", "row", "col"),
        P(("row", "layer"), "col"),
        P(("row", "layer")),
        P("col"),
    )
    return jax.shard_map(
        local, mesh=mesh, in_specs=placed, out_specs=P(("row", "layer"), "col"), check_vma=False
    )
```

profile of v0, /device:TPU:1, one launch (start us, length us, event | category | flops | bytes accessed | tf_op | source)
XLA Modules:
  0.0 286.8 jit_solution(3546155924513565021)
XLA Ops:
  6.5 0.0 copy-start
  6.5 0.0 copy-start.1
  6.5 0.0 copy-start.2
  6.5 0.0 all-gather.5.cloned.1.call-start
  6.5 0.7 all-gather.5.cloned.1.call-update
  7.3 0.0 all-gather.3.cloned.1.call-start
  7.3 0.7 all-gather.3.cloned.1.call-update
  8.0 0.0 all-reduce.2.cloned.1.call-start
  8.1 64.0 %all-gather.5.cloned.1.call-done = bf16[16,1024,128]{2,1,0:T(8,128)(2,1)} async-done(((bf16[16,128,128]{2,1,0:T(8,128)(2,1)}), bf16[16,1024,128]{2,1,0:T(8,128)(2,1)}) %all-gather.5.cloned.1.call-update) | async-done | bytes 4194320 | tf_op jit(solution)/shard_map/all_gather | solution.py:9
  72.1 147.7 %all-gather.3.cloned.1.call-done = bf16[16,1024,384]{2,1,0:T(8,128)(2,1)} async-done(((bf16[16,64,384]{2,1,0:T(8,128)(2,1)}), bf16[16,1024,384]{2,1,0:T(8,128)(2,1)}) %all-gather.3.cloned.1.call-update) | async-done | bytes 12582928 | tf_op jit(solution)/shard_map/all_gather | solution.py:11
  219.8 9.9 %convolution_bitcast_fusion = f32[384,128]{1,0:T(8,128)} fusion(bf16[16,1024,384]{2,1,0:T(8,128)(2,1)} %all-gather.3.cloned.1.call-done, bf16[16,1024,128]{2,1,0:T(8,128)(2,1)} %all-gather.5.cloned.1.call-done), kind=kOutput, calls=%fused_computation | convolution fusion | flops 1610612736 | bytes 16973824 | tf_op jit(solution)/shard_map/dot_general | solution.py:10
  229.7 0.0 all-reduce.2.cloned.1.call-update
  229.7 49.0 %all-reduce.2.cloned.1.call-done = f32[384,128]{1,0:T(8,128)} async-done(((f32[384,128]{1,0:T(8,128)}), f32[384,128]{1,0:T(8,128)}) %all-reduce.2.cloned.1.call-update) | async-done | bytes 196624 | tf_op jit(solution)/shard_map/psum | solution.py:17
  278.7 0.0 copy-done
  278.7 0.0 copy-done.1
  278.7 0.0 copy-done.2
  278.7 1.5 add_divide_fusion
Async XLA Ops:
  6.5 272.2 %copy-start = (bf16[96,128]{1,0:T(8,128)(2,1)S(1)}, bf16[96,128]{1,0:T(8,128)(2,1)}, u32[]{:S(2)}) copy-start(bf16[96,128]{1,0:T(8,128)(2,1)} %param.7) | copy-start | bytes 73732
  6.5 272.2 %copy-start.1 = (f32[128]{0:T(128)S(1)}, f32[128]{0:T(128)}, u32[]{:S(2)}) copy-start(f32[128]{0:T(128)} %param.9) | copy-start | bytes 1540
  6.5 272.2 %copy-start.2 = (f32[96]{0:T(128)S(1)}, f32[96]{0:T(128)}, u32[]{:S(2)}) copy-start(f32[96]{0:T(128)} %param.8) | copy-start | bytes 1156
  6.5 65.6 %all-gather.5.cloned.1.call-start = ((), (), s32[]{:S(2)}) async-start(), calls=%async_computation.1 | async-start | bytes 4718592 | tf_op jit(solution)/shard_map/all_gather | solution.py:9
  7.3 212.5 %all-gather.3.cloned.1.call-start = ((), (), s32[]{:S(2)}) async-start(), calls=%async_computation | async-start | bytes 13369344 | tf_op jit(solution)/shard_map/all_gather | solution.py:11
  8.0 270.7 %all-reduce.2.cloned.1.call-start = ((), (), s32[]{:S(2)}) async-start(), calls=%async_computation.2 | async-start | bytes 393216 | tf_op jit(solution)/shard_map/psum | solution.py:17
Sparse Core Ops, SparseCore 0:
  9.4 62.6 all-gather.4
  74.2 145.5 all-gather.2
  229.8 48.8 all-reduce.1
where the time goes:
time: 287 us
  waiting for transfers between devices  262 us (91%)
  between operations  13.1 us (5%)
  matrix products  9.89 us (3%)
    all_gather x1, waiting for transfers between devices, local(): lax.all_gather(integrals, 'col', axis=1, tiled=True)  148 us
    all_gather x1, waiting for transfers between devices, local(): gathered = lax.all_gather(amplitudes, 'row', axis=1, tiled=True)  64 us
    psum x1, waiting for transfers between devices, local(): summed_all = lax.psum(partial_sum, 'layer')  49 us
    dot_general x1, matrix products, local(): lax.dot_general(lax.all_gather(integrals, 'col', axis=1, tiled=True), gat...  9.89 us
  transfers between devices with their start and end apart: 3, of which 3 were waited for; matrix products, arithmetic and copies ran while one was open for 0% of the time, Pallas kernels for 0%

commit v1 on v0

--- a/solution.py
+++ b/solution.py
@@ -6,7 +6,13 @@
 
 def local(integrals, amplitudes, coulomb, row_gap, col_gap):
     contract = (((0, 1), (0, 1)), ((), ()))
-    gathered = lax.all_gather(amplitudes, "row", axis=1, tiled=True)
+    peers = lax.axis_size("row")
+    moving, parts = (amplitudes, [amplitudes])
+    for _ in range(peers - 1):
+        moving = lax.ppermute(moving, "row", [(i, (i + 1) % peers) for i in range(peers)])
+        parts.insert(0, moving)
+    line = jnp.concatenate(parts, axis=1)
+    gathered = jnp.roll(line, (lax.axis_index("row") + 1) * amplitudes.shape[1], axis=1)
     partial_sum = lax.dot_general(
         lax.all_gather(integrals, "col", axis=1, tiled=True),
         gathered,

time: 287 us -> 231 us (0.80)
  waiting for transfers between devices: 262 us -> 165 us
  local copies, waits for them, and re-layouts: 0.01 us -> 20 us
  starting transfers between devices: 0.08 us -> 19.1 us
    all_gather x1, waiting for transfers between devices: 148 us -> 40.1 us  [local(): lax.all_gather(integrals, 'col', axis=1, tiled=True)]
    ppermute x0 -> x7, waiting for transfers between devices: none -> 75 us  [local(): lax.ppermute(moving, 'row', [(i, (i + 1) % peers) for i in range(peers)])]
    all_gather x1 -> x0, waiting for transfers between devices: 64 us -> none  [local(): gathered = lax.all_gather(amplitudes, 'row', axis=1, tiled=True)]
    unnamed x6 -> x22, local copies, waits for them, and re-layouts: 0.01 us -> 19.1 us
    ppermute x0 -> x7, starting transfers between devices: none -> 19 us  [local(): lax.ppermute(moving, 'row', [(i, (i + 1) % peers) for i in range(peers)])]
  transfers between devices with their start and end apart: 3 -> 9, of which waited for: 3 -> 9; matrix products, arithmetic and copies ran while one was open for 0% -> 9% of each run, Pallas kernels for 0% -> 0%
where the time goes in v1:
time: 231 us; the launch traced here: 230 us
  waiting for transfers between devices  165 us (71%)
  local copies, waits for them, and re-layouts  20 us (9%)
  starting transfers between devices  19.1 us (8%)
  between operations  13.5 us (6%)
  matrix products  11.5 us (5%)
    ppermute x7, waiting for transfers between devices, local(): lax.ppermute(moving, 'row', [(i, (i + 1) % peers) for i in range(peers)])  75 us
    psum x1, waiting for transfers between devices, local(): summed_all = lax.psum(partial_sum, 'layer')  49 us
    all_gather x1, waiting for transfers between devices, local(): lax.all_gather(integrals, 'col', axis=1, tiled=True)  40.1 us
    unnamed x22, local copies, waits for them, and re-layouts  19.1 us
    ppermute x7, starting transfers between devices, local(): lax.ppermute(moving, 'row', [(i, (i + 1) % peers) for i in range(peers)])  19 us
    dot_general x1, matrix products, local(): lax.dot_general(lax.all_gather(integrals, 'col', axis=1, tiled=True), gat...  11.5 us
  transfers between devices with their start and end apart: 9, of which 9 were waited for; matrix products, arithmetic and copies ran while one was open for 9% of the time, Pallas kernels for 0%

profile of v1, /device:TPU:1, one launch (start us, length us, event | category | flops | bytes accessed | tf_op | source)
XLA Modules:
  0.0 230.4 jit_solution(1171871287431351955)
XLA Ops:
  6.5 0.0 all-gather.2.cloned.1.call-start
  6.5 0.7 all-gather.2.cloned.1.call-update
  7.3 0.0 all-reduce.2.cloned.1.call-start
  7.3 1.3 copy.11
  8.6 4.0 %collective-permute-start = (bf16[16,128,128]{1,2,0:T(8,128)(2,1)S(1)}, bf16[16,128,128]{1,2,0:T(8,128)(2,1)S(1)}, u32[]{:S(2)}, u32[]{:S(2)}) collective-permute-start(bf16[16,128,128]{1,2,0:T(8,128)(2,1)S(1)} %copy.11), channel_id=1, source_target_pairs={{0,64},{64,128},{128,192},{192,256},{256,320},{320,384},{384,448},... | collective-permute-start | bytes 1572872 | tf_op jit(solution)/shard_map/ppermute | solution.py:12
  12.7 8.4 %collective-permute-done = bf16[16,128,128]{1,2,0:T(8,128)(2,1)S(1)} collective-permute-done((bf16[16,128,128]{1,2,0:T(8,128)(2,1)S(1)}, bf16[16,128,128]{1,2,0:T(8,128)(2,1)S(1)}, u32[]{:S(2)}, u32[]{:S(2)}) %collective-permute-start) | collective-permute-done | bytes 524320 | tf_op jit(solution)/shard_map/ppermute | solution.py:12
  21.1 5.3 %collective-permute-start.1 = (bf16[16,128,128]{1,2,0:T(8,128)(2,1)S(1)}, bf16[16,128,128]{1,2,0:T(8,128)(2,1)S(1)}, u32[]{:S(2)}, u32[]{:S(2)}) collective-permute-start(bf16[16,128,128]{1,2,0:T(8,128)(2,1)S(1)} %collective-permute-done), channel_id=1, source_target_pairs={{0,64},{64,128},{128,192},{192,256},{256,320},{320,384},{384,448},... | collective-permute-start | bytes 1572872 | tf_op jit(solution)/shard_map/ppermute | solution.py:12
  26.4 11.7 %collective-permute-done.1 = bf16[16,128,128]{1,2,0:T(8,128)(2,1)S(1)} collective-permute-done((bf16[16,128,128]{1,2,0:T(8,128)(2,1)S(1)}, bf16[16,128,128]{1,2,0:T(8,128)(2,1)S(1)}, u32[]{:S(2)}, u32[]{:S(2)}) %collective-permute-start.1) | collective-permute-done | bytes 524320 | tf_op jit(solution)/shard_map/ppermute | solution.py:12
  38.2 2.0 collective-permute-start.2
  40.2 11.4 %collective-permute-done.2 = bf16[16,128,128]{1,2,0:T(8,128)(2,1)S(1)} collective-permute-done((bf16[16,128,128]{1,2,0:T(8,128)(2,1)S(1)}, bf16[16,128,128]{1,2,0:T(8,128)(2,1)S(1)}, u32[]{:S(2)}, u32[]{:S(2)}) %collective-permute-start.2) | collective-permute-done | bytes 524320 | tf_op jit(solution)/shard_map/ppermute | solution.py:12
  51.6 1.9 collective-permute-start.3
  53.5 10.3 %collective-permute-done.3 = bf16[16,128,128]{1,2,0:T(8,128)(2,1)S(1)} collective-permute-done((bf16[16,128,128]{1,2,0:T(8,128)(2,1)S(1)}, bf16[16,128,128]{1,2,0:T(8,128)(2,1)S(1)}, u32[]{:S(2)}, u32[]{:S(2)}) %collective-permute-start.3) | collective-permute-done | bytes 524320 | tf_op jit(solution)/shard_map/ppermute | solution.py:12
  63.8 1.9 collective-permute-start.4
  65.7 13.0 %collective-permute-done.4 = bf16[16,128,128]{1,2,0:T(8,128)(2,1)S(1)} collective-permute-done((bf16[16,128,128]{1,2,0:T(8,128)(2,1)S(1)}, bf16[16,128,128]{1,2,0:T(8,128)(2,1)S(1)}, u32[]{:S(2)}, u32[]{:S(2)}) %collective-permute-start.4) | collective-permute-done | bytes 524320 | tf_op jit(solution)/shard_map/ppermute | solution.py:12
  78.7 1.9 collective-permute-start.5
  80.6 10.4 %collective-permute-done.5 = bf16[16,128,128]{1,2,0:T(8,128)(2,1)} collective-permute-done((bf16[16,128,128]{1,2,0:T(8,128)(2,1)S(1)}, bf16[16,128,128]{1,2,0:T(8,128)(2,1)}, u32[]{:S(2)}, u32[]{:S(2)}) %collective-permute-start.5) | collective-permute-done | bytes 524320 | tf_op jit(solution)/shard_map/ppermute | solution.py:12
  91.0 1.9 collective-permute-start.6
  92.9 9.8 %collective-permute-done.6 = bf16[16,128,128]{1,2,0:T(8,128)(2,1)} collective-permute-done((bf16[16,128,128]{1,2,0:T(8,128)(2,1)}, bf16[16,128,128]{1,2,0:T(8,128)(2,1)}, u32[]{:S(2)}, u32[]{:S(2)}) %collective-permute-start.6) | collective-permute-done | bytes 524320 | tf_op jit(solution)/shard_map/ppermute | solution.py:12
  102.7 2.0 constant_dynamic-update-slice_fusion.15
  104.7 2.0 constant_dynamic-update-slice_fusion.14
  106.7 0.9 constant_dynamic-update-slice_fusion.13
  107.6 0.9 constant_dynamic-update-slice_fusion.12
  108.5 0.9 constant_dynamic-update-slice_fusion.11
  109.4 0.9 constant_dynamic-update-slice_fusion.10
  110.3 0.9 constant_dynamic-update-slice_fusion.9
  111.2 0.9 constant_dynamic-update-slice_fusion.8
  112.1 2.0 constant_dynamic-update-slice_fusion.7
  114.0 2.0 constant_dynamic-update-slice_fusion.6
  116.0 0.9 constant_dynamic-update-slice_fusion.5
  116.9 0.9 constant_dynamic-update-slice_fusion.4
  117.8 0.9 constant_dynamic-update-slice_fusion.3
  118.7 0.9 constant_dynamic-update-slice_fusion.2
  119.6 0.9 constant_dynamic-update-slice_fusion.1
  120.5 0.9 constant_dynamic-update-slice_fusion
  121.4 0.0 copy-start
  121.4 0.0 copy-start.1
  121.4 0.0 copy-start.2
  121.4 40.1 %all-gather.2.cloned.1.call-done = bf16[16,1024,384]{2,1,0:T(8,128)(2,1)} async-done(((bf16[16,64,384]{2,1,0:T(8,128)(2,1)}), bf16[16,1024,384]{2,1,0:T(8,128)(2,1)}) %all-gather.2.cloned.1.call-update) | async-done | bytes 12582928 | tf_op jit(solution)/shard_map/all_gather | solution.py:17
  161.5 11.5 %fusion.2 = f32[384,128]{1,0:T(8,128)} fusion(bf16[16,1024,384]{2,1,0:T(8,128)(2,1)} %all-gather.2.cloned.1.call-done, bf16[16,2048,128]{1,2,0:T(8,128)(2,1)} %constant_dynamic-update-slice_fusion, s32[]{:T(128)S(6)} %select_n.17), kind=kOutput, calls=%fused_computation.2 | convolution fusion | flops 1610612736 | bytes 16973828 | tf_op jit(solution)/shard_map/dot_general | solution.py:16
  173.0 0.0 all-reduce.2.cloned.1.call-update
  173.0 49.0 %all-reduce.2.cloned.1.call-done = f32[384,128]{1,0:T(8,128)} async-done(((f32[384,128]{1,0:T(8,128)}), f32[384,128]{1,0:T(8,128)}) %all-reduce.2.cloned.1.call-update) | async-done | bytes 196624 | tf_op jit(solution)/shard_map/psum | solution.py:23
  222.1 0.0 copy-done
  222.1 0.0 copy-done.1
  222.1 0.0 copy-done.2
  222.1 1.5 add_divide_fusion
Async XLA Ops:
  6.5 155.0 %all-gather.2.cloned.1.call-start = ((), (), s32[]{:S(2)}) async-start(), calls=%async_computation | async-start | bytes 13369344 | tf_op jit(solution)/shard_map/all_gather | solution.py:17
  7.3 214.8 %all-reduce.2.cloned.1.call-start = ((), (), s32[]{:S(2)}) async-start(), calls=%async_computation.1 | async-start | bytes 393216 | tf_op jit(solution)/shard_map/psum | solution.py:23
  8.6 12.5 %collective-permute-start = (bf16[16,128,128]{1,2,0:T(8,128)(2,1)S(1)}, bf16[16,128,128]{1,2,0:T(8,128)(2,1)S(1)}, u32[]{:S(2)}, u32[]{:S(2)}) collective-permute-start(bf16[16,128,128]{1,2,0:T(8,128)(2,1)S(1)} %copy.11), channel_id=1, source_target_pairs={{0,64},{64,128},{128,192},{192,256},{256,320},{320,384},{384,448},... | collective-permute-start | bytes 1572872 | tf_op jit(solution)/shard_map/ppermute | solution.py:12
  21.1 17.0 %collective-permute-start.1 = (bf16[16,128,128]{1,2,0:T(8,128)(2,1)S(1)}, bf16[16,128,128]{1,2,0:T(8,128)(2,1)S(1)}, u32[]{:S(2)}, u32[]{:S(2)}) collective-permute-start(bf16[16,128,128]{1,2,0:T(8,128)(2,1)S(1)} %collective-permute-done), channel_id=1, source_target_pairs={{0,64},{64,128},{128,192},{192,256},{256,320},{320,384},{384,448},... | collective-permute-start | bytes 1572872 | tf_op jit(solution)/shard_map/ppermute | solution.py:12
  38.2 13.4 %collective-permute-start.2 = (bf16[16,128,128]{1,2,0:T(8,128)(2,1)S(1)}, bf16[16,128,128]{1,2,0:T(8,128)(2,1)S(1)}, u32[]{:S(2)}, u32[]{:S(2)}) collective-permute-start(bf16[16,128,128]{1,2,0:T(8,128)(2,1)S(1)} %collective-permute-done.1), channel_id=1, source_target_pairs={{0,64},{64,128},{128,192},{192,256},{256,320},{320,384},{384,448},... | collective-permute-start | bytes 1572872 | tf_op jit(solution)/shard_map/ppermute | solution.py:12
  51.6 12.2 %collective-permute-start.3 = (bf16[16,128,128]{1,2,0:T(8,128)(2,1)S(1)}, bf16[16,128,128]{1,2,0:T(8,128)(2,1)S(1)}, u32[]{:S(2)}, u32[]{:S(2)}) collective-permute-start(bf16[16,128,128]{1,2,0:T(8,128)(2,1)S(1)} %collective-permute-done.2), channel_id=1, source_target_pairs={{0,64},{64,128},{128,192},{192,256},{256,320},{320,384},{384,448},... | collective-permute-start | bytes 1572872 | tf_op jit(solution)/shard_map/ppermute | solution.py:12
  63.8 14.9 %collective-permute-start.4 = (bf16[16,128,128]{1,2,0:T(8,128)(2,1)S(1)}, bf16[16,128,128]{1,2,0:T(8,128)(2,1)S(1)}, u32[]{:S(2)}, u32[]{:S(2)}) collective-permute-start(bf16[16,128,128]{1,2,0:T(8,128)(2,1)S(1)} %collective-permute-done.3), channel_id=1, source_target_pairs={{0,64},{64,128},{128,192},{192,256},{256,320},{320,384},{384,448},... | collective-permute-start | bytes 1572872 | tf_op jit(solution)/shard_map/ppermute | solution.py:12
  78.7 12.3 %collective-permute-start.5 = (bf16[16,128,128]{1,2,0:T(8,128)(2,1)S(1)}, bf16[16,128,128]{1,2,0:T(8,128)(2,1)}, u32[]{:S(2)}, u32[]{:S(2)}) collective-permute-start(bf16[16,128,128]{1,2,0:T(8,128)(2,1)S(1)} %collective-permute-done.4), channel_id=1, source_target_pairs={{0,64},{64,128},{128,192},{192,256},{256,320},{320,384},{384,448},... | collective-permute-start | bytes 1572872 | tf_op jit(solution)/shard_map/ppermute | solution.py:12
  91.0 11.7 %collective-permute-start.6 = (bf16[16,128,128]{1,2,0:T(8,128)(2,1)}, bf16[16,128,128]{1,2,0:T(8,128)(2,1)}, u32[]{:S(2)}, u32[]{:S(2)}) collective-permute-start(bf16[16,128,128]{1,2,0:T(8,128)(2,1)} %collective-permute-done.5), channel_id=1, source_target_pairs={{0,64},{64,128},{128,192},{192,256},{256,320},{320,384},{384,448},... | collective-permute-start | bytes 1572872 | tf_op jit(solution)/shard_map/ppermute | solution.py:12
  121.4 100.7 %copy-start = (bf16[96,128]{1,0:T(8,128)(2,1)S(1)}, bf16[96,128]{1,0:T(8,128)(2,1)}, u32[]{:S(2)}) copy-start(bf16[96,128]{1,0:T(8,128)(2,1)} %param.7) | copy-start | bytes 73732
  121.4 100.7 %copy-start.1 = (f32[128]{0:T(128)S(1)}, f32[128]{0:T(128)}, u32[]{:S(2)}) copy-start(f32[128]{0:T(128)} %param.9) | copy-start | bytes 1540
  121.4 100.7 %copy-start.2 = (f32[96]{0:T(128)S(1)}, f32[96]{0:T(128)}, u32[]{:S(2)}) copy-start(f32[96]{0:T(128)} %param.8) | copy-start | bytes 1156
Sparse Core Ops, SparseCore 0:
  9.4 151.9 all-gather.1
  173.1 48.8 all-reduce.1
